TPU v7x, 32 devices: a whole 2x2x4 slice. The times are simulated.
32 devices in a mesh: gx: 8 (over z, y), gy: 4 (over x, core).
Axes of the slice: x: 2, y: 2, z: 4, core: 2. Of those that a mesh axis runs over, the one named last changes fastest.
Arguments:
- populations: float32 [27, 64, 8192], P(None, 'gx', 'gy'), may hold values from 0.6 to 1.4
- marker_site: int32 [4, 16384], P(None, ('gx', 'gy')), may hold values from 0 to 63, as said below
- marker_frac: float32 [3, 16384], P(None, ('gx', 'gy')), may hold values from 0 to 1
- marker_force: float32 [3, 16384], P(None, ('gx', 'gy')), may hold values from -2 to 2
- marker_count: int32 [8], P('gx'), may hold values from 256 to 2048, as said below
Outputs:
- populations_next: float32 [27, 64, 8192], P(None, 'gx', 'gy')
Inputs may be any that keep to these rules, and one draw needn't show every extreme that they name: `marker_site`: row 0 is the owning tile's row, below 4; rows 1, 2, 3 are cell offsets inside that tile, below 8, 32 and 64. The owning tile lies in the column of the slot. A column's live markers fill its first marker_count slots; some column is full in every draw.
All inputs are finite; a program needn't handle non-finite values.
Results may differ from a plain program's by a relative error of at most 0.0003.
Values sent between devices are 32-bit elements; how exact they have to be, the bound alone decides.
A program may use at most 64 MiB of HBM per device.

v0:
```python
import jax
import jax.numpy as jnp
from jax import lax
from jax.sharding import PartitionSpec as P

NZ = 64


RELAX_RATE = 1.8
LINE_WEIGHTS = (1.0 / 6.0, 2.0 / 3.0, 1.0 / 6.0)


def extended_2(cells, sides, width):
    for axis, dim in sides:
        count = lax.axis_size(axis)
        head = lax.slice_in_dim(cells, 0, width, axis=dim)
        tail = lax.slice_in_dim(cells, cells.shape[dim] - width, cells.shape[dim], axis=dim)
        cells = jnp.concatenate(
            [
                lax.ppermute(tail, axis, [(i, (i + 1) % count) for i in range(count)]),
                cells,
                lax.ppermute(head, axis, [((i + 1) % count, i) for i in range(count)]),
            ],
            axis=dim,
        )
    return cells


def passed_along(block, axis, distance):
    devices = range(lax.axis_size(axis))
    route = [((i - distance) % len(devices), i) for i in devices]
    return lax.ppermute(block, axis, route)


def gaussian_moment(labels, covariance):
    if len(labels) == 0:
        return None
    result = None
    for position in range(1, len(labels)):
        remaining = labels[1:position] + labels[position + 1 :]
        lower_label = min(labels[0], labels[position])
        upper_label = max(labels[0], labels[position])
        product = covariance[lower_label, upper_label]
        inner = gaussian_moment(remaining, covariance)
        if inner is not None:
            product = product * inner
        result = product if result is None else result + product
    return result


def forward_line(lower_pop, centre_pop, upper_pop, velocity):
    summed = lower_pop + centre_pop + upper_pop
    first_order = upper_pop - lower_pop - velocity * summed
    second_order = (
        upper_pop * (1.0 - velocity) * (1.0 - velocity)
        + lower_pop * (1.0 + velocity) * (1.0 + velocity)
        + centre_pop * velocity * velocity
    )
    return (summed, first_order, second_order)


def backward_line(zeroth, first_order, second_order, velocity):
    square = velocity * velocity
    centre_pop = zeroth * (1.0 - square) - 2.0 * velocity * first_order - second_order
    lower_pop = 0.5 * (
        zeroth * (square - velocity) + first_order * (2.0 * velocity - 1.0) + second_order
    )
    upper_pop = 0.5 * (
        zeroth * (square + velocity) + first_order * (2.0 * velocity + 1.0) + second_order
    )
    return (lower_pop, centre_pop, upper_pop)


def place_slot(axis_pick, slot, outer, inner):
    if axis_pick == 0:
        return (slot, outer, inner)
    if axis_pick == 1:
        return (outer, slot, inner)
    return (outer, inner, slot)


def transform(grid, velocity, axis_pick, line_fn):
    result = dict(grid)
    for outer in range(3):
        for inner in range(3):
            triples = [place_slot(axis_pick, slot, outer, inner) for slot in range(3)]
            outputs = line_fn(grid[triples[0]], grid[triples[1]], grid[triples[2]], velocity)
            for slot in range(3):
                result[triples[slot]] = outputs[slot]
    return result


def collide(populations, force):
    grid = {}
    weights = []
    for index in range(27):
        triple = (index // 9, index // 3 % 3, index % 3)
        weight = LINE_WEIGHTS[triple[0]] * LINE_WEIGHTS[triple[1]] * LINE_WEIGHTS[triple[2]]
        weights.append(weight)
        grid[triple] = weight * populations[index]
    density = sum(grid.values())
    velocity = []
    for axis_pick in range(3):
        momentum = sum((grid[triple] for triple in grid if triple[axis_pick] == 2)) - sum(
            (grid[triple] for triple in grid if triple[axis_pick] == 0)
        )
        velocity.append((momentum + 0.5 * force[axis_pick]) / density)
    moments = transform(grid, velocity[2], 2, forward_line)
    moments = transform(moments, velocity[1], 1, forward_line)
    moments = transform(moments, velocity[0], 0, forward_line)
    second = {
        (0, 0): moments[2, 0, 0],
        (1, 1): moments[0, 2, 0],
        (2, 2): moments[0, 0, 2],
        (0, 1): moments[1, 1, 0],
        (0, 2): moments[1, 0, 1],
        (1, 2): moments[0, 1, 1],
    }
    trace_third = (second[0, 0] + second[1, 1] + second[2, 2]) / 3.0
    covariance = {}
    for entry_pair in second:
        if entry_pair[0] == entry_pair[1]:
            relaxed = density / 3.0 + (1.0 - RELAX_RATE) * (second[entry_pair] - trace_third)
        else:
            relaxed = (1.0 - RELAX_RATE) * second[entry_pair]
        covariance[entry_pair] = relaxed / density
    post_moments = {}
    for triple in moments:
        total_order = triple[0] + triple[1] + triple[2]
        labels = [0] * triple[0] + [1] * triple[1] + [2] * triple[2]
        if total_order == 0:
            post_moments[triple] = density
        elif total_order == 1:
            post_moments[triple] = 0.5 * force[labels[0]]
        elif total_order % 2 == 1:
            post_moments[triple] = jnp.zeros_like(density)
        else:
            post_moments[triple] = density * gaussian_moment(labels, covariance)
    restored = transform(post_moments, velocity[0], 0, backward_line)
    restored = transform(restored, velocity[1], 1, backward_line)
    restored = transform(restored, velocity[2], 2, backward_line)
    return jnp.stack(
        [restored[index // 9, index // 3 % 3, index % 3] / weights[index] for index in range(27)], 0
    )


def z_roll(block, offset, lane_z):
    if offset == 0:
        return block
    plain = jnp.roll(block, offset, axis=-1)
    wrapped = jnp.roll(block, offset - offset * NZ, axis=-1)
    edge = lane_z == 0 if offset == 1 else lane_z == NZ - 1
    return jnp.where(edge, wrapped, plain)


def stream_faces(post, width_x, lane_count, lane_z):
    padded = extended_2(post, (("gx", 1),), 1)
    padded = extended_2(padded, (("gy", 2),), NZ)
    read = []
    for index in range(27):
        shift_x = index // 9 - 1
        shift_y = index // 3 % 3 - 1
        shift_z = index % 3 - 1
        start_y = (1 - shift_y) * NZ
        piece = padded[index, 1 - shift_x : 1 - shift_x + width_x, start_y : start_y + lane_count]
        read.append(z_roll(piece, shift_z, lane_z))
    return jnp.stack(read, 0)


def spread_block(
    site_rows, frac_rows, force_rows, live_mask, tile_y, y_offset, y_rows, column_rows, width_x
):
    x_cells = jnp.arange(width_x + 1, dtype=jnp.int32)
    z_cells = jnp.arange(NZ, dtype=jnp.int32)
    y_cells = jnp.arange(y_rows, dtype=jnp.int32)
    frac_x = frac_rows[0][:, None]
    frac_y = frac_rows[1][:, None]
    frac_z = frac_rows[2][:, None]
    start_x = site_rows[1][:, None]
    start_z = site_rows[3][:, None]
    weight_x = (x_cells[None, :] == start_x).astype(jnp.float32) * (1.0 - frac_x) + (
        x_cells[None, :] == start_x + 1
    ).astype(jnp.float32) * frac_x
    weight_z = (z_cells[None, :] == start_z).astype(jnp.float32) * (1.0 - frac_z) + (
        z_cells[None, :] == (start_z + 1) % NZ
    ).astype(jnp.float32) * frac_z
    weight_y = jnp.zeros((site_rows.shape[1], y_rows), jnp.float32)
    for step_y in (0, 1):
        local_y = (site_rows[0] * tile_y + site_rows[2] + step_y - y_offset) % column_rows
        factor_y = frac_y if step_y else 1.0 - frac_y
        weight_y = weight_y + (y_cells[None, :] == local_y[:, None]).astype(jnp.float32) * factor_y
    scaled = force_rows.T * live_mask[:, None]
    carried = scaled[:, :, None, None] * weight_x[:, None, :, None] * weight_z[:, None, None, :]
    carried = carried.reshape(site_rows.shape[1], 3 * (width_x + 1) * NZ)
    return jnp.dot(
        weight_y.T, carried, precision=lax.Precision.HIGHEST, preferred_element_type=jnp.float32
    )


def per_device(populations, marker_site, marker_frac, marker_force, marker_count):
    width_x = populations.shape[1]
    lane_count = populations.shape[2]
    tile_y = lane_count // NZ
    tile_rows = lax.axis_size("gy")
    column_rows = tile_y * tile_rows
    my_row = lax.axis_index("gy")
    column_count = marker_count[0]
    own_slots = marker_site.shape[1]
    row_width = 3 * (width_x + 1) * NZ
    gathered_site, gathered_frac, gathered_force = (
        lax.all_gather(marker_site, "gy", axis=1, tiled=True),
        lax.all_gather(marker_frac, "gy", axis=1, tiled=True),
        lax.all_gather(marker_force, "gy", axis=1, tiled=True),
    )

    def add_block(turn, total):
        start = turn * own_slots
        site_rows = lax.dynamic_slice_in_dim(gathered_site, start, own_slots, 1)
        frac_rows = lax.dynamic_slice_in_dim(gathered_frac, start, own_slots, 1)
        force_rows = lax.dynamic_slice_in_dim(gathered_force, start, own_slots, 1)
        slot_rank = start + jnp.arange(own_slots, dtype=jnp.int32)
        live_mask = (slot_rank < column_count).astype(jnp.float32)
        return total + spread_block(
            site_rows,
            frac_rows,
            force_rows,
            live_mask,
            tile_y,
            my_row * tile_y,
            tile_y,
            column_rows,
            width_x,
        )

    owned = lax.fori_loop(0, tile_rows, add_block, jnp.zeros((tile_y, row_width), jnp.float32))
    extended = (
        owned.reshape(tile_y, 3, width_x + 1, NZ)
        .transpose(1, 2, 0, 3)
        .reshape(3, width_x + 1, lane_count)
    )
    rim_plane = passed_along(extended[:, width_x], "gx", 1)
    force = jnp.concatenate([(extended[:, 0] + rim_plane)[:, None], extended[:, 1:width_x]], axis=1)
    post = collide(populations, force)
    lane_z = jnp.arange(lane_count, dtype=jnp.int32) % NZ
    return stream_faces(post, width_x, lane_count, lane_z)


def solution(mesh):
    in_specs = (
        P(None, "gx", "gy"),
        P(None, ("gx", "gy")),
        P(None, ("gx", "gy")),
        P(None, ("gx", "gy")),
        P("gx"),
    )
    out_specs = P(None, "gx", "gy")
    return jax.shard_map(
        per_device, mesh=mesh, in_specs=in_specs, out_specs=out_specs, check_vma=False
    )
```

profile of v0, /device:TPU:0, one launch (start us, length us, event | category | flops | bytes accessed | tf_op | source)
XLA Modules:
  0.0 93.2 jit_solution(4755230872810844511)
XLA Ops:
  0.0 8.0 %all_gather.10 = f32[3,2048]{1,0:T(4,128)} all-gather(f32[3,512]{1,0:T(4,128)} %param.9), channel_id=1, replica_groups=mesh['gx'=8,'gy'=4] {'gy'}, dimensions={1}, use_global_device_ids=true | all-gather | bytes 30720 | tf_op jit(solution)/shard_map/all_gather | solution.py:212
  8.0 5.8 %all_gather.11 = f32[3,2048]{1,0:T(4,128)} all-gather(f32[3,512]{1,0:T(4,128)} %param.10), channel_id=1, replica_groups=mesh['gx'=8,'gy'=4] {'gy'}, dimensions={1}, use_global_device_ids=true | all-gather | bytes 30720 | tf_op jit(solution)/shard_map/all_gather | solution.py:213
  13.9 6.3 %all_gather.9 = s32[4,2048]{1,0:T(4,128)} all-gather(s32[4,512]{1,0:T(4,128)} %param.8), channel_id=1, replica_groups=mesh['gx'=8,'gy'=4] {'gy'}, dimensions={1}, use_global_device_ids=true | all-gather | bytes 40960 | tf_op jit(solution)/shard_map/all_gather | solution.py:211
  20.2 34.5 %while.17 = (s32[]{:T(128)}, f32[32,1728]{1,0:T(8,128)}, s32[4,2048]{1,0:T(4,128)}, s32[]{:T(128)}, f32[3,2048]{1,0:T(4,128)}, /*index=5*/f32[3,2048]{1,0:T(4,12...) while((s32[]{:T(128)}, f32[32,1728]{1,0:T(8,128)}, ...), condition=%wide.region_1.2_spmd.clone, body=%wide.region_0.1_spmd.clone.sunk | while | flops 341041664 | bytes 8038673 | solution.py:235
  20.2 0.9 broadcast_subtract_fusion.8
  21.1 0.9 fusion.188
  24.0 4.1 %convolution_add_fusion.2 = f32[32,1728]{1,0:T(8,128)} fusion(f32[512,1728]{0,1:T(8,128)S(1)} %bitcast.734, f32[32,1728]{1,0:T(8,128)} %get-tuple-element.494, f32[512]{0:T(512)S(1)} %bitcast.737, s32[512]{0:T(512)S(1)} %get-tuple-element.477, f32[512]{0:T(512)S(1)} %broadcast_subtract_fusion.11, s32[512]{0:T(512)S(1)} %get-tuple-element.478, ...), kind=kOutput, calls=%fused_computation.clone.1 | convolution fusion | flops 339931136 | bytes 3989505 | tf_op jit(solution)/shard_map/while/body/eval_jaxpr/dot_general | solution.py:195
  28.1 0.9 broadcast_subtract_fusion.8
  29.1 0.9 fusion.188
  31.9 5.1 %convolution_add_fusion.2 = f32[32,1728]{1,0:T(8,128)} fusion(f32[512,1728]{0,1:T(8,128)S(1)} %bitcast.734, f32[32,1728]{1,0:T(8,128)} %get-tuple-element.494, f32[512]{0:T(512)S(1)} %bitcast.737, s32[512]{0:T(512)S(1)} %get-tuple-element.477, f32[512]{0:T(512)S(1)} %broadcast_subtract_fusion.11, s32[512]{0:T(512)S(1)} %get-tuple-element.478, ...), kind=kOutput, calls=%fused_computation.clone.1 | convolution fusion | flops 339931136 | bytes 3989505 | tf_op jit(solution)/shard_map/while/body/eval_jaxpr/dot_general | solution.py:195
  37.0 0.9 broadcast_subtract_fusion.8
  37.9 0.9 fusion.188
  40.8 5.1 %convolution_add_fusion.2 = f32[32,1728]{1,0:T(8,128)} fusion(f32[512,1728]{0,1:T(8,128)S(1)} %bitcast.734, f32[32,1728]{1,0:T(8,128)} %get-tuple-element.494, f32[512]{0:T(512)S(1)} %bitcast.737, s32[512]{0:T(512)S(1)} %get-tuple-element.477, f32[512]{0:T(512)S(1)} %broadcast_subtract_fusion.11, s32[512]{0:T(512)S(1)} %get-tuple-element.478, ...), kind=kOutput, calls=%fused_computation.clone.1 | convolution fusion | flops 339931136 | bytes 3989505 | tf_op jit(solution)/shard_map/while/body/eval_jaxpr/dot_general | solution.py:195
  45.9 0.9 broadcast_subtract_fusion.8
  49.6 5.1 %convolution_add_fusion.2 = f32[32,1728]{1,0:T(8,128)} fusion(f32[512,1728]{0,1:T(8,128)S(1)} %bitcast.734, f32[32,1728]{1,0:T(8,128)} %get-tuple-element.494, f32[512]{0:T(512)S(1)} %bitcast.737, s32[512]{0:T(512)S(1)} %get-tuple-element.477, f32[512]{0:T(512)S(1)} %broadcast_subtract_fusion.11, s32[512]{0:T(512)S(1)} %get-tuple-element.478, ...), kind=kOutput, calls=%fused_computation.clone.1 | convolution fusion | flops 339931136 | bytes 3989505 | tf_op jit(solution)/shard_map/while/body/eval_jaxpr/dot_general | solution.py:195
  54.7 1.2 %reshape.1765 = f32[32,3,9,64]{3,2,1,0:T(8,128)S(1)} reshape(f32[32,1728]{1,0:T(8,128)} %get-tuple-element.211) | data formatting | bytes 442368 | tf_op jit(solution)/shard_map/reshape | solution.py:237
  56.4 1.6 %collective-permute-start = (f32[3,2048]{1,0:T(4,128)S(1)}, f32[3,2048]{1,0:T(4,128)S(1)}, u32[]{:S(2)}, u32[]{:S(2)}) collective-permute-start(f32[3,2048]{1,0:T(4,128)S(1)} %slice_bitcast_fusion.36), channel_id=1, source_target_pairs={{28,0},{0,4},{4,8},{8,12},{12,16},{16,20},{20,24},{24,28},{29,1},{... | collective-permute-start | bytes 73736 | tf_op jit(solution)/shard_map/ppermute | solution.py:32
  58.2 4.8 %collective-permute-done = f32[3,2048]{1,0:T(4,128)S(1)} collective-permute-done((f32[3,2048]{1,0:T(4,128)S(1)}, f32[3,2048]{1,0:T(4,128)S(1)}, u32[]{:S(2)}, u32[]{:S(2)}) %collective-permute-start) | collective-permute-done | bytes 24608 | tf_op jit(solution)/shard_map/ppermute | solution.py:32
  67.8 4.7 %collective-permute-start.2 = (f32[27,1,2048]{2,1,0:T(1,128)S(1)}, f32[27,1,2048]{2,1,0:T(1,128)S(1)}, u32[]{:S(2)}, u32[]{:S(2)}) collective-permute-start(f32[27,1,2048]{2,1,0:T(1,128)S(1)} %get-tuple-element.401), channel_id=1, source_target_pairs={{4,0},{8,4},{12,8},{16,12},{20,16},{24,20},{28,24},{0,28},{5,1},{9... | collective-permute-start | bytes 663560 | tf_op jit(solution)/shard_map/ppermute | solution.py:22
  72.6 4.6 %collective-permute-done.1 = f32[27,1,2048]{2,1,0:T(1,128)S(1)} collective-permute-done((f32[27,1,2048]{2,1,0:T(1,128)S(1)}, f32[27,1,2048]{2,1,0:T(1,128)S(1)}, u32[]{:S(2)}, u32[]{:S(2)}) %collective-permute-start.1) | collective-permute-done | bytes 221216 | tf_op jit(solution)/shard_map/ppermute | solution.py:20
  77.2 2.0 %collective-permute-done.2 = f32[27,1,2048]{2,1,0:T(1,128)S(1)} collective-permute-done((f32[27,1,2048]{2,1,0:T(1,128)S(1)}, f32[27,1,2048]{2,1,0:T(1,128)S(1)}, u32[]{:S(2)}, u32[]{:S(2)}) %collective-permute-start.2) | collective-permute-done | bytes 221216 | tf_op jit(solution)/shard_map/ppermute | solution.py:22
  80.0 5.0 %collective-permute-done.3 = f32[27,10,64]{2,1,0:T(8,128)S(1)} collective-permute-done((f32[27,10,64]{2,1,0:T(8,128)S(1)}, f32[27,10,64]{2,1,0:T(8,128)S(1)}, u32[]{:S(2)}, u32[]{:S(2)}) %collective-permute-start.3) | collective-permute-done | bytes 69152 | tf_op jit(solution)/shard_map/ppermute | solution.py:22
  85.3 1.2 %collective-permute-done.4 = f32[27,10,64]{2,1,0:T(8,128)S(1)} collective-permute-done((f32[27,10,64]{2,1,0:T(8,128)S(1)}, f32[27,10,64]{2,1,0:T(8,128)S(1)}, u32[]{:S(2)}, u32[]{:S(2)}) %collective-permute-start.4) | collective-permute-done | bytes 69152 | tf_op jit(solution)/shard_map/ppermute | solution.py:20
  91.5 1.0 %copy-done.1 = f32[27,8,2048]{2,1,0:T(8,128)} copy-done((f32[27,8,2048]{2,1,0:T(8,128)}, f32[27,8,2048]{2,1,0:T(8,128)S(1)}, u32[]{:S(2)}) %copy-start.1) | copy-done | bytes 1769496
  (200 shorter events, 20.2 us)
Async XLA Ops:
  54.7 3.2 %copy-start = (f32[27,8,2048]{2,1,0:T(8,128)S(1)}, f32[27,8,2048]{2,1,0:T(8,128)}, u32[]{:S(2)}) copy-start(f32[27,8,2048]{2,1,0:T(8,128)} %param.7) | copy-start | bytes 5308420
  56.4 6.7 %collective-permute-start = (f32[3,2048]{1,0:T(4,128)S(1)}, f32[3,2048]{1,0:T(4,128)S(1)}, u32[]{:S(2)}, u32[]{:S(2)}) collective-permute-start(f32[3,2048]{1,0:T(4,128)S(1)} %slice_bitcast_fusion.36), channel_id=1, source_target_pairs={{28,0},{0,4},{4,8},{8,12},{12,16},{16,20},{20,24},{24,28},{29,1},{... | collective-permute-start | bytes 73736 | tf_op jit(solution)/shard_map/ppermute | solution.py:32
  67.7 9.5 %collective-permute-start.1 = (f32[27,1,2048]{2,1,0:T(1,128)S(1)}, f32[27,1,2048]{2,1,0:T(1,128)S(1)}, u32[]{:S(2)}, u32[]{:S(2)}) collective-permute-start(f32[27,1,2048]{2,1,0:T(1,128)S(1)} %get-tuple-element.400), channel_id=1, source_target_pairs={{0,4},{4,8},{8,12},{12,16},{16,20},{20,24},{24,28},{28,0},{1,5},{5... | collective-permute-start | bytes 663560 | tf_op jit(solution)/shard_map/ppermute | solution.py:20
  67.8 11.4 %collective-permute-start.2 = (f32[27,1,2048]{2,1,0:T(1,128)S(1)}, f32[27,1,2048]{2,1,0:T(1,128)S(1)}, u32[]{:S(2)}, u32[]{:S(2)}) collective-permute-start(f32[27,1,2048]{2,1,0:T(1,128)S(1)} %get-tuple-element.401), channel_id=1, source_target_pairs={{4,0},{8,4},{12,8},{16,12},{20,16},{24,20},{28,24},{0,28},{5,1},{9... | collective-permute-start | bytes 663560 | tf_op jit(solution)/shard_map/ppermute | solution.py:22
  79.4 5.5 %collective-permute-start.3 = (f32[27,10,64]{2,1,0:T(8,128)S(1)}, f32[27,10,64]{2,1,0:T(8,128)S(1)}, u32[]{:S(2)}, u32[]{:S(2)}) collective-permute-start(f32[27,10,64]{2,1,0:T(8,128)S(1)} %get-tuple-element.394), channel_id=1, source_target_pairs={{1,0},{2,1},{3,2},{0,3},{5,4},{6,5},{7,6},{4,7},{9,8},{10,9},{11,1... | collective-permute-start | bytes 207368 | tf_op jit(solution)/shard_map/ppermute | solution.py:22
  79.5 7.0 %collective-permute-start.4 = (f32[27,10,64]{2,1,0:T(8,128)S(1)}, f32[27,10,64]{2,1,0:T(8,128)S(1)}, u32[]{:S(2)}, u32[]{:S(2)}) collective-permute-start(f32[27,10,64]{2,1,0:T(8,128)S(1)} %get-tuple-element.393), channel_id=1, source_target_pairs={{0,1},{1,2},{2,3},{3,0},{4,5},{5,6},{6,7},{7,4},{8,9},{9,10},{10,1... | collective-permute-start | bytes 207368 | tf_op jit(solution)/shard_map/ppermute | solution.py:20
  91.3 1.2 %copy-start.1 = (f32[27,8,2048]{2,1,0:T(8,128)}, f32[27,8,2048]{2,1,0:T(8,128)S(1)}, u32[]{:S(2)}) copy-start(f32[27,8,2048]{2,1,0:T(8,128)S(1)} %get-tuple-element.377) | copy-start | bytes 5308420
where the time goes:
time: 94.4 us; the launch traced here: 93.2 us
  blocking collectives  20.2 us (21%)
  matrix products  19.4 us (21%)
  other arithmetic  18.9 us (20%)
  waiting for transfers between devices  17.6 us (19%)
  local copies, waits for them, and re-layouts  9.28 us (10%)
  starting transfers between devices  6.88 us (7%)
    dot_general x4, matrix products, spread_block(): jnp.dot(weight_y.T, carried, precision=lax.Precision.HIGHEST, preferred_e...  19.4 us
    all_gather x1, blocking collectives, per_device(): lax.all_gather(marker_frac, 'gy', axis=1, tiled=True)  8.03 us
    ppermute x2, waiting for transfers between devices, extended_2(): lax.ppermute(head, axis, [((i + 1) % count, i) for i in range(count)])  6.95 us
    all_gather x1, blocking collectives, per_device(): lax.all_gather(marker_site, 'gy', axis=1, tiled=True)  6.34 us
    all_gather x1, blocking collectives, per_device(): lax.all_gather(marker_force, 'gy', axis=1, tiled=True)  5.84 us
    ppermute x2, waiting for transfers between devices, extended_2(): lax.ppermute(tail, axis, [(i, (i + 1) % count) for i in range(count)])  5.83 us
    ppermute x1, waiting for transfers between devices, passed_along(): return lax.ppermute(block, axis, route)  4.85 us
    ppermute x2, starting transfers between devices, extended_2(): lax.ppermute(head, axis, [((i + 1) % count, i) for i in range(count)])  4.77 us
  transfers between devices with their start and end apart: 5, of which 5 were waited for; matrix products, arithmetic and copies ran while one was open for 1% of the time, Pallas kernels for 0%

commit v1 on v0

v1 whole, which is shorter than its diff:
```python
import functools

import jax
import jax.numpy as jnp
from jax import lax
from jax.experimental import pallas as pl
from jax.experimental.pallas import tpu as pltpu
from jax.sharding import PartitionSpec as P

NZ = 64
LANES = 128
RELAX_RATE = 1.8
MESH = pl.DeviceIdType.MESH
F32 = jnp.float32
BF16 = jnp.bfloat16


def backward_line(zeroth, first, second, velocity):
    if zeroth is None:
        low = first
    elif first is None:
        low = zeroth * velocity
    else:
        low = zeroth * velocity + first
    high = None
    if low is not None:
        high = velocity * (low if first is None else low + first)
    if second is not None:
        high = second if high is None else high + second
    if low is None:
        lower = upper = high
    else:
        lower, upper = high - low, high + low
    if high is None:
        centre = 0.5 * zeroth
    elif zeroth is None:
        centre = -0.5 * high
    else:
        centre = 0.5 * (zeroth - high)
    return lower, centre, upper


def backward(grid, velocity, axis):
    result = {}
    for outer in range(3):
        for inner in range(3):
            keys = []
            for slot in range(3):
                key = [outer, inner]
                key.insert(axis, slot)
                keys.append(tuple(key))
            made = backward_line(*[grid.get(key) for key in keys], velocity)
            for key, value in zip(keys, made):
                result[key] = value
    return result


def raw_moments(load):
    rows = []
    for i in range(3):
        sums, diffs, evens = [], [], []
        for j in range(3):
            low, mid, high = load(9 * i + 3 * j), load(9 * i + 3 * j + 1), load(9 * i + 3 * j + 2)
            even = low + high
            evens.append(even)
            sums.append(even + 4.0 * mid)
            diffs.append(high - low)
        even = sums[0] + sums[2]
        rows.append(
            (
                even + 4.0 * sums[1],
                sums[2] - sums[0],
                even,
                diffs[0] + diffs[2] + 4.0 * diffs[1],
                diffs[2] - diffs[0],
                evens[0] + evens[2] + 4.0 * evens[1],
            )
        )

    def total(at):
        return rows[0][at] + rows[2][at] + 4.0 * rows[1][at]

    def first(at):
        return rows[2][at] - rows[0][at]

    made = (
        total(0),
        first(0),
        total(1),
        total(3),
        rows[0][0] + rows[2][0],
        total(2),
        total(5),
        first(1),
        first(3),
        total(4),
    )
    return [value * (1.0 / 216.0) for value in made]


def collided(moments, force):
    density, jx, jy, jz, cxx, cyy, czz, cxy, cxz, cyz = moments
    gx, gy, gz = [0.5 * value for value in force]
    inverse = 1.0 / density
    velocity = ((jx + gx) * inverse, (jy + gy) * inverse, (jz + gz) * inverse)
    cxx = cxx + (gx * gx - jx * jx) * inverse
    cyy = cyy + (gy * gy - jy * jy) * inverse
    czz = czz + (gz * gz - jz * jz) * inverse
    cxy = cxy + (gx * gy - jx * jy) * inverse
    cxz = cxz + (gx * gz - jx * jz) * inverse
    cyz = cyz + (gy * gz - jy * jz) * inverse
    keep = 1.0 - RELAX_RATE
    scaled = keep * inverse
    base = (1.0 / 3.0) - (cxx + cyy + czz) * (scaled * (1.0 / 3.0))
    sxx, syy, szz = base + cxx * scaled, base + cyy * scaled, base + czz * scaled
    sxy, sxz, syz = cxy * scaled, cxz * scaled, cyz * scaled
    mass = 27.0 * density
    dxy, dxz, dyz = 2.0 * sxy, 2.0 * sxz, 2.0 * syz
    pxy = sxx * syy + dxy * sxy
    qxy, qxz, qyz = dxy * sxy, dxz * sxz, dyz * syz
    grid = {
        (0, 0, 0): mass,
        (1, 0, 0): 27.0 * gx,
        (0, 1, 0): 27.0 * gy,
        (0, 0, 1): 27.0 * gz,
        (2, 0, 0): mass * sxx,
        (0, 2, 0): mass * syy,
        (0, 0, 2): mass * szz,
        (1, 1, 0): mass * sxy,
        (1, 0, 1): mass * sxz,
        (0, 1, 1): mass * syz,
        (2, 2, 0): mass * pxy,
        (2, 0, 2): mass * (sxx * szz + qxz),
        (0, 2, 2): mass * (syy * szz + qyz),
        (2, 1, 1): mass * (sxx * syz + dxy * sxz),
        (1, 2, 1): mass * (syy * sxz + dxy * syz),
        (1, 1, 2): mass * (szz * sxy + dxz * syz),
        (2, 2, 2): mass * (pxy * szz + sxx * qyz + syy * qxz + 4.0 * (dxy * (sxz * syz))),
    }
    for axis in range(3):
        grid = backward(grid, velocity[axis], axis)
    return grid


def split(value):
    high = value.astype(BF16).astype(F32)
    return high, value - high


def step_kernel(
    n_x, n_y, pop, site, frac, force, count, out,
    in_v, mom, slots, lhs_hi, lhs_lo, rhs_hi, rhs_lo, acc, rim_s, rim_r, out_v,
    face_p, face_m, got_p, got_m, side_p, side_m, cor,
    in_sem, mark_s, mark_r, rim_sem, face_sem, side_sem, cor_s, cor_r, out_sem,
):
    me_x, me_y = lax.axis_index("gx"), lax.axis_index("gy")
    tiles = in_v.shape[0]
    tile_y = 2 * tiles
    own = site.shape[1]
    right, left = lax.rem(me_x + 1, n_x), lax.rem(me_x + n_x - 1, n_x)
    above, below = lax.rem(me_y + 1, n_y), lax.rem(me_y + n_y - 1, n_y)

    def in_copy(t):
        lanes = pl.ds(pl.multiple_of(t * LANES, LANES), LANES)
        return pltpu.make_async_copy(pop.at[:, :, lanes], in_v.at[t], in_sem.at[t])

    @pl.loop(0, tiles)
    def _(t):
        in_copy(t).start()

    barrier = pltpu.get_barrier_semaphore()
    near = [(me_x, lax.rem(me_y + k, n_y)) for k in range(1, n_y)]
    near += [(a, b) for a in (right, left) for b in (me_y, above, below)]
    for device in near:
        pl.semaphore_signal(barrier, inc=1, device_id=device, device_id_type=MESH)

    rank = me_y * own + lax.broadcasted_iota(jnp.int32, (3, own), 1)
    slots[0, 0:4, :] = site[...].astype(F32)
    slots[0, 4:7, :] = frac[...]
    slots[0, 7:10, :] = jnp.where(rank < count[0], force[...], 0.0)

    pl.semaphore_wait(barrier, len(near))

    def mark_copy(k):
        return pltpu.make_async_remote_copy(
            src_ref=slots.at[0],
            dst_ref=slots.at[k],
            send_sem=mark_s.at[k],
            recv_sem=mark_r.at[k],
            device_id=(me_x, lax.rem(me_y + k, n_y)),
            device_id_type=MESH,
        )

    for k in range(1, n_y):
        mark_copy(k).start()

    def spread(k):
        def row(at):
            return jnp.broadcast_to(slots[k, at : at + 1, :], (8, own))

        cells = lax.broadcasted_iota(jnp.int32, (8, own), 0).astype(F32)
        at_y = row(0) * float(tile_y) + row(2) - (me_y * tile_y).astype(F32)
        at_y = jnp.where(at_y < 0.0, at_y + float(tile_y * n_y), at_y)
        next_y = at_y + 1.0
        next_y = jnp.where(next_y == float(tile_y * n_y), 0.0, next_y)
        at_x, at_z = row(1), row(3)
        next_z = jnp.where(at_z == NZ - 1.0, 0.0, at_z + 1.0)
        frac_x, frac_y, frac_z = row(4), row(5), row(6)
        weight_x = jnp.where(
            cells == at_x, 1.0 - frac_x, jnp.where(cells == at_x + 1.0, frac_x, 0.0)
        )
        first = split(weight_x * (1.0 - frac_y))
        second = split(weight_x * frac_y)
        refs = (lhs_hi, lhs_lo)
        for pair in range(tile_y // 2):
            picked = [[], []]
            for y in (2 * pair, 2 * pair + 1):
                hit, hit_next = at_y == float(y), next_y == float(y)
                for part in range(2):
                    picked[part].append(
                        jnp.where(hit, first[part], jnp.where(hit_next, second[part], 0.0))
                    )
            for part in range(2):
                refs[part][16 * pair : 16 * pair + 16, :] = jnp.concatenate(picked[part], 0).astype(BF16)
        rim = jnp.where(at_x == 7.0, frac_x, 0.0)
        first = split(rim * (1.0 - frac_y))
        second = split(rim * frac_y)
        for pair in range(tile_y // 16):
            picked = [[], []]
            for half in range(2):
                rows = cells + float(16 * pair + 8 * half)
                hit, hit_next = at_y == rows, next_y == rows
                for part in range(2):
                    picked[part].append(
                        jnp.where(hit, first[part], jnp.where(hit_next, second[part], 0.0))
                    )
            base = 8 * tile_y + 16 * pair
            for part in range(2):
                refs[part][base : base + 16, :] = jnp.concatenate(picked[part], 0).astype(BF16)
        refs = (rhs_hi, rhs_lo)
        for axis in range(3):
            amount = row(7 + axis)
            first = split(amount * (1.0 - frac_z))
            second = split(amount * frac_z)
            for pair in range(NZ // 16):
                picked = [[], []]
                for half in range(2):
                    rows = cells + float(16 * pair + 8 * half)
                    hit, hit_next = at_z == rows, next_z == rows
                    for part in range(2):
                        picked[part].append(
                            jnp.where(hit, first[part], jnp.where(hit_next, second[part], 0.0))
                        )
                base = axis * NZ + 16 * pair
                for part in range(2):
                    refs[part][base : base + 16, :] = jnp.concatenate(picked[part], 0).astype(BF16)

        def product(a, b):
            return lax.dot_general(
                a[...], b[...], (((1,), (1,)), ((), ())), preferred_element_type=F32
            )

        return product(lhs_hi, rhs_hi) + product(lhs_hi, rhs_lo) + product(lhs_lo, rhs_hi)

    width = 3 * NZ
    acc[:, 0:width] = spread(0)

    @pl.loop(1, n_y)
    def _(k):
        mark_copy(k).wait_recv()
        acc[:, 0:width] += spread(k)

    rim_s[...] = acc[8 * tile_y :, :]
    rim_copy = pltpu.make_async_remote_copy(
        src_ref=rim_s, dst_ref=rim_r, send_sem=rim_sem.at[0], recv_sem=rim_sem.at[1],
        device_id=(right, me_y), device_id_type=MESH,
    )
    rim_copy.start()

    @pl.loop(0, tiles)
    def _(t):
        in_copy(t).wait()
        for at, value in enumerate(raw_moments(lambda q: in_v[t, q])):
            mom[t, at] = value

    rim_copy.wait_recv()
    for y in range(tile_y):
        acc[8 * y : 8 * y + 1, :] += rim_r[y : y + 1, :]

    lane = lax.broadcasted_iota(jnp.int32, (8, LANES), 1)
    lower_half = lane < NZ
    z_low = (lane == 0) | (lane == NZ)
    z_high = (lane == NZ - 1) | (lane == LANES - 1)

    @pl.loop(0, tiles)
    def _(t):
        even = acc[pl.ds(pl.multiple_of(16 * t, 16), 8), :]
        odd = acc[pl.ds(pl.multiple_of(16 * t + 8, 8), 8), :]
        a0, a1, b0, b1 = even[:, :LANES], even[:, LANES:], odd[:, :LANES], odd[:, LANES:]
        forces = (
            jnp.where(lower_half, a0, pltpu.roll(b0, NZ, 1)),
            jnp.where(lower_half, pltpu.roll(a0, NZ, 1), b0),
            jnp.where(lower_half, a1, pltpu.roll(b1, NZ, 1)),
        )
        post = collided([mom[t, at] for at in range(10)], forces)
        for i in range(3):
            for j in range(3):
                for k in range(3):
                    q = 9 * i + 3 * j + k
                    value = post[i, j, k]
                    if k == 1:
                        if j != 1:
                            value = pltpu.roll(value, NZ, 1)
                    else:
                        near_by, edge, far = (1, z_low, NZ + 1) if k == 2 else (LANES - 1, z_high, NZ - 1)
                        plain, wrapped = pltpu.roll(value, near_by, 1), pltpu.roll(value, far, 1)
                        if j != 1:
                            plain, wrapped = wrapped, plain
                        value = jnp.where(edge, wrapped, plain)
                    moved = value
                    if i == 2:
                        moved = pltpu.roll(value, 1, 0)
                    elif i == 0:
                        moved = pltpu.roll(value, 7, 0)
                    line = moved if i == 2 else value
                    face = (face_m, None, face_p)[i]
                    at = 3 * j + k
                    if j == 1:
                        out_v[q, t + 1] = moved
                        if i != 1:
                            face[t + 1, at : at + 1, :] = line[0:1, :]
                    else:
                        low_at, high_at = (t + 2, t + 1) if j == 2 else (t + 1, t)
                        out_v[q, low_at, :, 0:NZ] = moved[:, 0:NZ]
                        out_v[q, high_at, :, NZ:] = moved[:, NZ:]
                        if i != 1:
                            face[low_at, at : at + 1, 0:NZ] = line[0:1, 0:NZ]
                            face[high_at, at : at + 1, NZ:] = line[0:1, NZ:]

    def send(src, dst, sems, device):
        return pltpu.make_async_remote_copy(
            src_ref=src, dst_ref=dst, send_sem=sems[0], recv_sem=sems[1],
            device_id=device, device_id_type=MESH,
        )

    inner = pl.ds(1, tiles)
    faces = [
        send(face_p.at[inner], got_p, (face_sem.at[0], face_sem.at[1]), (right, me_y)),
        send(face_m.at[inner], got_m, (face_sem.at[2], face_sem.at[3]), (left, me_y)),
    ]
    corners = []
    for at, (buffer, tile, device) in enumerate(
        (
            (face_p, tiles + 1, (right, above)),
            (face_p, 0, (right, below)),
            (face_m, tiles + 1, (left, above)),
            (face_m, 0, (left, below)),
        )
    ):
        corners.append(send(buffer.at[tile], cor.at[at], (cor_s.at[at], cor_r.at[at]), device))
    sides = []
    for i in range(3):
        sides.append(
            send(out_v.at[pl.ds(9 * i + 6, 3), tiles + 1], side_p.at[pl.ds(3 * i, 3)],
                 (side_sem.at[0, i], side_sem.at[1, i]), (me_x, above))
        )
        sides.append(
            send(out_v.at[pl.ds(9 * i, 3), 0], side_m.at[pl.ds(3 * i, 3)],
                 (side_sem.at[2, i], side_sem.at[3, i]), (me_x, below))
        )
    for copy in faces + corners + sides:
        copy.start()

    for copy in sides:
        copy.wait_recv()
    for i in range(3):
        for k in range(3):
            out_v[9 * i + 6 + k, 1, :, 0:NZ] = side_p[3 * i + k, :, 0:NZ]
            out_v[9 * i + k, tiles, :, NZ:] = side_m[3 * i + k, :, NZ:]

    def out_copy(t, group):
        lanes = pl.ds(pl.multiple_of(t * LANES, LANES), LANES)
        rows = pl.ds(9 * group, 9)
        return pltpu.make_async_copy(
            out_v.at[rows, t + 1], out.at[rows, :, lanes], out_sem.at[group, t]
        )

    @pl.loop(0, tiles)
    def _(t):
        out_copy(t, 1).start()

    for copy in corners:
        copy.wait_recv()
    for copy in faces:
        copy.wait_recv()
    for k in range(3):
        got_p[0, 6 + k : 7 + k, 0:NZ] = cor[0, 6 + k : 7 + k, 0:NZ]
        got_p[tiles - 1, k : k + 1, NZ:] = cor[1, k : k + 1, NZ:]
        got_m[0, 6 + k : 7 + k, 0:NZ] = cor[2, 6 + k : 7 + k, 0:NZ]
        got_m[tiles - 1, k : k + 1, NZ:] = cor[3, k : k + 1, NZ:]

    @pl.loop(0, tiles)
    def _(t):
        for at in range(9):
            out_v[18 + at, t + 1, 0:1, :] = got_p[t, at : at + 1, :]
            out_v[at, t + 1, 7:8, :] = got_m[t, at : at + 1, :]
        out_copy(t, 0).start()
        out_copy(t, 2).start()

    for k in range(1, n_y):
        mark_copy(k).wait_send()
    rim_copy.wait_send()
    for copy in faces + corners + sides:
        copy.wait_send()

    @pl.loop(0, tiles)
    def _(t):
        for group in range(3):
            out_copy(t, group).wait()


def per_device(n_x, n_y, populations, marker_site, marker_frac, marker_force, marker_count):
    tiles = populations.shape[2] // LANES
    own = marker_site.shape[1]
    tile_y = 2 * tiles
    rows = 9 * tile_y
    width = 3 * NZ
    dma = pltpu.SemaphoreType.DMA
    vmem = pl.BlockSpec(memory_space=pltpu.VMEM)
    anywhere = pl.BlockSpec(memory_space=pl.ANY)
    return pl.pallas_call(
        functools.partial(step_kernel, n_x, n_y),
        out_shape=jax.ShapeDtypeStruct(populations.shape, F32),
        in_specs=[anywhere, vmem, vmem, vmem, pl.BlockSpec(memory_space=pltpu.SMEM)],
        out_specs=anywhere,
        scratch_shapes=[
            pltpu.VMEM((tiles, 27, 8, LANES), F32),
            pltpu.VMEM((tiles, 10, 8, LANES), F32),
            pltpu.VMEM((n_y, 10, own), F32),
            pltpu.VMEM((rows, own), BF16),
            pltpu.VMEM((rows, own), BF16),
            pltpu.VMEM((width, own), BF16),
            pltpu.VMEM((width, own), BF16),
            pltpu.VMEM((rows, 2 * LANES), F32),
            pltpu.VMEM((tile_y, 2 * LANES), F32),
            pltpu.VMEM((tile_y, 2 * LANES), F32),
            pltpu.VMEM((27, tiles + 2, 8, LANES), F32),
            pltpu.VMEM((tiles + 2, 9, LANES), F32),
            pltpu.VMEM((tiles + 2, 9, LANES), F32),
            pltpu.VMEM((tiles, 9, LANES), F32),
            pltpu.VMEM((tiles, 9, LANES), F32),
            pltpu.VMEM((9, 8, LANES), F32),
            pltpu.VMEM((9, 8, LANES), F32),
            pltpu.VMEM((4, 9, LANES), F32),
            dma((tiles,)),
            dma((n_y,)),
            dma((n_y,)),
            dma((2,)),
            dma((4,)),
            dma((4, 3)),
            dma((4,)),
            dma((4,)),
            dma((3, tiles)),
        ],
        compiler_params=pltpu.CompilerParams(
            collective_id=0, has_side_effects=True, vmem_limit_bytes=40 * 1024 * 1024
        ),
    )(populations, marker_site, marker_frac, marker_force, marker_count)


def solution(mesh):
    in_specs = (
        P(None, "gx", "gy"),
        P(None, ("gx", "gy")),
        P(None, ("gx", "gy")),
        P(None, ("gx", "gy")),
        P("gx"),
    )
    return jax.shard_map(
        functools.partial(per_device, mesh.shape["gx"], mesh.shape["gy"]),
        mesh=mesh,
        in_specs=in_specs,
        out_specs=P(None, "gx", "gy"),
        check_vma=False,
    )
```

time: 94.4 us -> 29 us (0.31)
  Pallas kernels: 0 us -> 23.3 us
  blocking collectives: 20.2 us -> 0 us
  matrix products: 19.4 us -> 0 us
  other arithmetic: 18.9 us -> 0 us
  waiting for transfers between devices: 17.6 us -> 0 us
  starting transfers between devices: 6.88 us -> 0 us
  local copies, waits for them, and re-layouts: 9.28 us -> 4.77 us
    pallas_call x0 -> x1, Pallas kernels: none -> 23.3 us  [per_device(): pl.pallas_call(functools.partial(step_kernel, n_x, n_y), out_shape=jax.Sh...]
    all_gather x3 -> x0, blocking collectives: 20.2 us -> none  [the longest x1 8.03 us: per_device(): lax.all_gather(marker_frac, 'gy', axis=1, tiled=True)]
    dot_general x4 -> x0, matrix products: 19.4 us -> none  [spread_block(): jnp.dot(weight_y.T, carried, precision=lax.Precision.HIGHEST, preferred_e...]
    ppermute x5 -> x0, waiting for transfers between devices: 17.6 us -> none  [the longest x2 6.95 us: extended_2(): lax.ppermute(head, axis, [((i + 1) % count, i) for i in range(count)])]
    ppermute x5 -> x0, starting transfers between devices: 6.88 us -> none  [the longest x2 4.77 us: extended_2(): lax.ppermute(head, axis, [((i + 1) % count, i) for i in range(count)])]
    mul x12 -> x0, other arithmetic: 4.64 us -> none  [the longest x4 2.83 us: spread_block(): scaled = force_rows.T * live_mask[:, None]]
    slice x6 -> x0, local copies, waits for them, and re-layouts: 3.9 us -> none  [the longest x4 3.57 us: spread_block(): frac_y = frac_rows[1][:, None]]
    sub x20 -> x0, other arithmetic: 3.75 us -> none  [the longest x8 3.71 us: spread_block(): site_rows[0] * tile_y + site_rows[2] + step_y - y_offset]
  transfers between devices with their start and end apart: 5 -> 0, of which waited for: 5 -> 0; matrix products, arithmetic and copies ran while one was open for 1% -> 0% of each run, Pallas kernels for 0% -> 0%
where the time goes in v1:
time: 29 us; the launch traced here: 28.7 us
  Pallas kernels  23.3 us (80%)
  local copies, waits for them, and re-layouts  4.77 us (16%)
  between operations  0.67 us (2%)
    pallas_call x1, Pallas kernels, per_device(): pl.pallas_call(functools.partial(step_kernel, n_x, n_y), out_shape=jax.Sh...  23.3 us
    unnamed x9, local copies, waits for them, and re-layouts  4.77 us

profile of v1, /device:TPU:0, one launch (start us, length us, event | category | flops | bytes accessed | tf_op | source)
XLA Modules:
  0.0 28.7 jit_solution(683087514100912513)
XLA Ops:
  0.7 0.0 copy-start
  0.7 1.5 %copy-done = f32[27,8,2048]{2,1,0:T(8,128)S(1)} copy-done((f32[27,8,2048]{2,1,0:T(8,128)S(1)}, f32[27,8,2048]{2,1,0:T(8,128)}, u32[]{:S(2)}) %copy-start) | copy-done | bytes 1769496
  2.1 0.0 copy-start.1
  2.1 0.7 %copy-done.1 = s32[4,512]{1,0:T(4,128)S(1)} copy-done((s32[4,512]{1,0:T(4,128)S(1)}, s32[4,512]{1,0:T(4,128)}, u32[]{:S(2)}) %copy-start.1) | copy-done | bytes 8216
  2.8 0.0 copy-start.2
  2.8 0.7 %copy-done.2 = f32[3,512]{1,0:T(4,128)S(1)} copy-done((f32[3,512]{1,0:T(4,128)S(1)}, f32[3,512]{1,0:T(4,128)}, u32[]{:S(2)}) %copy-start.2) | copy-done | bytes 6168
  3.5 0.0 copy-start.3
  3.5 0.7 %copy-done.3 = f32[3,512]{1,0:T(4,128)S(1)} copy-done((f32[3,512]{1,0:T(4,128)S(1)}, f32[3,512]{1,0:T(4,128)}, u32[]{:S(2)}) %copy-start.3) | copy-done | bytes 6168
  4.2 23.3 %shard_map.55 = f32[27,8,2048]{2,1,0:T(8,128)S(1)} custom-call(f32[27,8,2048]{2,1,0:T(8,128)S(1)} %copy-done, s32[4,512]{1,0:T(4,128)S(1)} %copy-done.1, f32[3,512]{1,0:T(4,128)S(1)} %copy-done.2, f32[3,512]{1,0:T(4,128)S(1)} %copy-done.3, s32[1]{0:T(128)S(6)} %copy.7.count), custom_call_target="tpu_custom_call" | custom-call | tf_op jit(solution)/shard_map/pallas_call | solution.py:431
  27.5 1.2 %copy.8 = f32[27,8,2048]{2,1,0:T(8,128)} copy(f32[27,8,2048]{2,1,0:T(8,128)S(1)} %shard_map.55) | data formatting | bytes 3538944
Async XLA Ops:
  0.7 1.5 %copy-start = (f32[27,8,2048]{2,1,0:T(8,128)S(1)}, f32[27,8,2048]{2,1,0:T(8,128)}, u32[]{:S(2)}) copy-start(f32[27,8,2048]{2,1,0:T(8,128)} %pop.1) | copy-start | bytes 5308420
  2.1 0.7 %copy-start.1 = (s32[4,512]{1,0:T(4,128)S(1)}, s32[4,512]{1,0:T(4,128)}, u32[]{:S(2)}) copy-start(s32[4,512]{1,0:T(4,128)} %site.1) | copy-start | bytes 24580
  2.8 0.7 %copy-start.2 = (f32[3,512]{1,0:T(4,128)S(1)}, f32[3,512]{1,0:T(4,128)}, u32[]{:S(2)}) copy-start(f32[3,512]{1,0:T(4,128)} %frac.1) | copy-start | bytes 18436
  3.5 0.7 %copy-start.3 = (f32[3,512]{1,0:T(4,128)S(1)}, f32[3,512]{1,0:T(4,128)}, u32[]{:S(2)}) copy-start(f32[3,512]{1,0:T(4,128)} %force.1) | copy-start | bytes 18436

commit v2 on v1

--- a/solution.py
+++ b/solution.py
@@ -148,10 +148,10 @@
 
 
 def step_kernel(
-    n_x, n_y, pop, site, frac, force, count, out,
-    in_v, mom, slots, lhs_hi, lhs_lo, rhs_hi, rhs_lo, acc, rim_s, rim_r, out_v,
+    n_x, n_y, pop, site_h, frac_h, force_h, count, out,
+    site, frac, force, in_v, mom, slots, lhs_hi, lhs_lo, rhs_hi, rhs_lo, acc, rim_s, rim_r, out_v,
     face_p, face_m, got_p, got_m, side_p, side_m, cor,
-    in_sem, mark_s, mark_r, rim_sem, face_sem, side_sem, cor_s, cor_r, out_sem,
+    own_sem, in_sem, mark_s, mark_r, rim_sem, face_sem, side_sem, cor_s, cor_r, out_sem,
 ):
     me_x, me_y = lax.axis_index("gx"), lax.axis_index("gy")
     tiles = in_v.shape[0]
@@ -164,9 +164,12 @@
         lanes = pl.ds(pl.multiple_of(t * LANES, LANES), LANES)
         return pltpu.make_async_copy(pop.at[:, :, lanes], in_v.at[t], in_sem.at[t])
 
-    @pl.loop(0, tiles)
-    def _(t):
-        in_copy(t).start()
+    fetches = [
+        pltpu.make_async_copy(src, dst, own_sem.at[at])
+        for at, (src, dst) in enumerate(((site_h, site), (frac_h, frac), (force_h, force)))
+    ]
+    for copy in fetches:
+        copy.start()
 
     barrier = pltpu.get_barrier_semaphore()
     near = [(me_x, lax.rem(me_y + k, n_y)) for k in range(1, n_y)]
@@ -174,6 +177,12 @@
     for device in near:
         pl.semaphore_signal(barrier, inc=1, device_id=device, device_id_type=MESH)
 
+    @pl.loop(0, tiles)
+    def _(t):
+        in_copy(t).start()
+
+    for copy in fetches:
+        copy.wait()
     rank = me_y * own + lax.broadcasted_iota(jnp.int32, (3, own), 1)
     slots[0, 0:4, :] = site[...].astype(F32)
     slots[0, 4:7, :] = frac[...]
@@ -292,8 +301,7 @@
     z_low = (lane == 0) | (lane == NZ)
     z_high = (lane == NZ - 1) | (lane == LANES - 1)
 
-    @pl.loop(0, tiles)
-    def _(t):
+    def tile_step(t):
         even = acc[pl.ds(pl.multiple_of(16 * t, 16), 8), :]
         odd = acc[pl.ds(pl.multiple_of(16 * t + 8, 8), 8), :]
         a0, a1, b0, b1 = even[:, :LANES], even[:, LANES:], odd[:, :LANES], odd[:, LANES:]
@@ -343,11 +351,6 @@
             device_id=device, device_id_type=MESH,
         )
 
-    inner = pl.ds(1, tiles)
-    faces = [
-        send(face_p.at[inner], got_p, (face_sem.at[0], face_sem.at[1]), (right, me_y)),
-        send(face_m.at[inner], got_m, (face_sem.at[2], face_sem.at[3]), (left, me_y)),
-    ]
     corners = []
     for at, (buffer, tile, device) in enumerate(
         (
@@ -368,8 +371,32 @@
             send(out_v.at[pl.ds(9 * i, 3), 0], side_m.at[pl.ds(3 * i, 3)],
                  (side_sem.at[2, i], side_sem.at[3, i]), (me_x, below))
         )
-    for copy in faces + corners + sides:
+    @pl.loop(0, 2)
+    def _(end):
+        tile_step(end * (tiles - 1))
+
+    for copy in corners + sides:
         copy.start()
+
+    faces = []
+    begin, source = 1, 1
+    for part in range(3):
+        stop = 1 + (part + 1) * (tiles - 2) // 3
+
+        @pl.loop(begin, stop)
+        def _(t):
+            tile_step(t)
+
+        end = tiles + 1 if part == 2 else stop
+        rows, places = pl.ds(source, end - source), pl.ds(source - 1, end - source)
+        for at, (buffer, got, device) in enumerate(
+            ((face_p, got_p, (right, me_y)), (face_m, got_m, (left, me_y)))
+        ):
+            sems = (face_sem.at[2 * at, part], face_sem.at[2 * at + 1, part])
+            faces.append(send(buffer.at[rows], got.at[places], sems, device))
+        faces[-2].start()
+        faces[-1].start()
+        begin, source = stop, end
 
     for copy in sides:
         copy.wait_recv()
@@ -387,7 +414,13 @@
 
     @pl.loop(0, tiles)
     def _(t):
-        out_copy(t, 1).start()
+        for group in range(3):
+            out_copy(t, group).start()
+
+    @pl.loop(0, tiles)
+    def _(t):
+        for group in range(3):
+            out_copy(t, group).wait()
 
     for copy in corners:
         copy.wait_recv()
@@ -401,22 +434,16 @@
 
     @pl.loop(0, tiles)
     def _(t):
+        lanes = pl.ds(pl.multiple_of(t * LANES, LANES), LANES)
         for at in range(9):
-            out_v[18 + at, t + 1, 0:1, :] = got_p[t, at : at + 1, :]
-            out_v[at, t + 1, 7:8, :] = got_m[t, at : at + 1, :]
-        out_copy(t, 0).start()
-        out_copy(t, 2).start()
+            out[18 + at, 0:1, lanes] = got_p[t, at : at + 1, :]
+            out[at, 7:8, lanes] = got_m[t, at : at + 1, :]
 
     for k in range(1, n_y):
         mark_copy(k).wait_send()
     rim_copy.wait_send()
     for copy in faces + corners + sides:
         copy.wait_send()
-
-    @pl.loop(0, tiles)
-    def _(t):
-        for group in range(3):
-            out_copy(t, group).wait()
 
 
 def per_device(n_x, n_y, populations, marker_site, marker_frac, marker_force, marker_count):
@@ -426,14 +453,16 @@
     rows = 9 * tile_y
     width = 3 * NZ
     dma = pltpu.SemaphoreType.DMA
-    vmem = pl.BlockSpec(memory_space=pltpu.VMEM)
-    anywhere = pl.BlockSpec(memory_space=pl.ANY)
+    hbm = pl.BlockSpec(memory_space=pltpu.HBM)
     return pl.pallas_call(
         functools.partial(step_kernel, n_x, n_y),
         out_shape=jax.ShapeDtypeStruct(populations.shape, F32),
-        in_specs=[anywhere, vmem, vmem, vmem, pl.BlockSpec(memory_space=pltpu.SMEM)],
-        out_specs=anywhere,
+        in_specs=[hbm, hbm, hbm, hbm, pl.BlockSpec(memory_space=pltpu.SMEM)],
+        out_specs=pl.BlockSpec(memory_space=pltpu.VMEM),
         scratch_shapes=[
+            pltpu.VMEM((4, own), jnp.int32),
+            pltpu.VMEM((3, own), F32),
+            pltpu.VMEM((3, own), F32),
             pltpu.VMEM((tiles, 27, 8, LANES), F32),
             pltpu.VMEM((tiles, 10, 8, LANES), F32),
             pltpu.VMEM((n_y, 10, own), F32),
@@ -452,11 +481,12 @@
             pltpu.VMEM((9, 8, LANES), F32),
             pltpu.VMEM((9, 8, LANES), F32),
             pltpu.VMEM((4, 9, LANES), F32),
+            dma((3,)),
             dma((tiles,)),
             dma((n_y,)),
             dma((n_y,)),
             dma((2,)),
-            dma((4,)),
+            dma((4, 3)),
             dma((4, 3)),
             dma((4,)),
             dma((4,)),
@@ -465,7 +495,7 @@
         compiler_params=pltpu.CompilerParams(
             collective_id=0, has_side_effects=True, vmem_limit_bytes=40 * 1024 * 1024
         ),
-    )(populations, marker_site, marker_frac, marker_force, marker_count)
+    )(*[pltpu.with_memory_space_constraint(value, pltpu.HBM) for value in (populations, marker_site, marker_frac, marker_force)], marker_count)
 
 
 def solution(mesh):

time: 29 us -> 23.6 us (0.81)
  local copies, waits for them, and re-layouts: 4.77 us -> 1.21 us
  Pallas kernels: 23.3 us -> 21.5 us
    unnamed x9 -> x1, local copies, waits for them, and re-layouts: 4.77 us -> 1.21 us
    pallas_call x1, Pallas kernels: 23.3 us -> 21.5 us  [per_device(): pl.pallas_call(functools.partial(step_kernel, n_x, n_y), out_shape=jax.Sh...]
where the time goes in v2:
time: 23.6 us; the launch traced here: 23.4 us
  Pallas kernels  21.5 us (91%)
  local copies, waits for them, and re-layouts  1.21 us (5%)
  between operations  0.66 us (3%)
    pallas_call x1, Pallas kernels, per_device(): pl.pallas_call(functools.partial(step_kernel, n_x, n_y), out_shape=jax.Sh...  21.5 us
    unnamed x1, local copies, waits for them, and re-layouts  1.21 us

profile of v2, /device:TPU:0, one launch (start us, length us, event | category | flops | bytes accessed | tf_op | source)
XLA Modules:
  0.0 23.4 jit_solution(5873728199770141499)
XLA Ops:
  0.7 21.5 %shard_map.55 = f32[27,8,2048]{2,1,0:T(8,128)S(1)} custom-call(f32[27,8,2048]{2,1,0:T(8,128)} %pop.1, s32[4,512]{1,0:T(4,128)} %site_h.1, f32[3,512]{1,0:T(4,128)} %frac_h.1, f32[3,512]{1,0:T(4,128)} %force_h.1, s32[1]{0:T(128)S(6)} %copy.7.count), custom_call_target="tpu_custom_call" | custom-call | tf_op jit(solution)/shard_map/pallas_call | solution.py:457
  22.2 1.2 %copy.8 = f32[27,8,2048]{2,1,0:T(8,128)} copy(f32[27,8,2048]{2,1,0:T(8,128)S(1)} %shard_map.55) | data formatting | bytes 3538944

commit v3 on v2

--- a/solution.py
+++ b/solution.py
@@ -149,9 +149,9 @@
 
 def step_kernel(
     n_x, n_y, pop, site_h, frac_h, force_h, count, out,
-    site, frac, force, in_v, mom, slots, lhs_hi, lhs_lo, rhs_hi, rhs_lo, acc, rim_s, rim_r, out_v,
+    site, frac, force, in_v, mom, slots, lhs_hi, lhs_lo, rhs_hi, rhs_lo, acc, rim_r, out_v,
     face_p, face_m, got_p, got_m, side_p, side_m, cor,
-    own_sem, in_sem, mark_s, mark_r, rim_sem, face_sem, side_sem, cor_s, cor_r, out_sem,
+    own_sem, in_sem, mark_s, mark_r, face_sem, side_sem, cor_s, cor_r, out_sem,
 ):
     me_x, me_y = lax.axis_index("gx"), lax.axis_index("gy")
     tiles = in_v.shape[0]
@@ -173,7 +173,7 @@
 
     barrier = pltpu.get_barrier_semaphore()
     near = [(me_x, lax.rem(me_y + k, n_y)) for k in range(1, n_y)]
-    near += [(a, b) for a in (right, left) for b in (me_y, above, below)]
+    near += [(a, lax.rem(me_y + k, n_y)) for a in (right, left) for k in range(n_y)]
     for device in near:
         pl.semaphore_signal(barrier, inc=1, device_id=device, device_id_type=MESH)
 
@@ -196,14 +196,20 @@
             dst_ref=slots.at[k],
             send_sem=mark_s.at[k],
             recv_sem=mark_r.at[k],
-            device_id=(me_x, lax.rem(me_y + k, n_y)),
+            device_id=(me_x if k < n_y else right, lax.rem(me_y + k, n_y)),
             device_id_type=MESH,
         )
 
-    for k in range(1, n_y):
+    for k in range(1, 2 * n_y):
         mark_copy(k).start()
 
-    def spread(k):
+    def slot_wait(k):
+        pltpu.make_async_remote_copy(
+            src_ref=slots.at[0], dst_ref=slots.at[k], send_sem=mark_s.at[k], recv_sem=mark_r.at[k],
+            device_id=(left, me_y), device_id_type=MESH,
+        ).wait_recv()
+
+    def spread(k, own_column):
         def row(at):
             return jnp.broadcast_to(slots[k, at : at + 1, :], (8, own))
 
@@ -221,7 +227,7 @@
         first = split(weight_x * (1.0 - frac_y))
         second = split(weight_x * frac_y)
         refs = (lhs_hi, lhs_lo)
-        for pair in range(tile_y // 2):
+        for pair in range(tile_y // 2 if own_column else 0):
             picked = [[], []]
             for y in (2 * pair, 2 * pair + 1):
                 hit, hit_next = at_y == float(y), next_y == float(y)
@@ -234,7 +240,7 @@
         rim = jnp.where(at_x == 7.0, frac_x, 0.0)
         first = split(rim * (1.0 - frac_y))
         second = split(rim * frac_y)
-        for pair in range(tile_y // 16):
+        for pair in range(0 if own_column else tile_y // 16):
             picked = [[], []]
             for half in range(2):
                 rows = cells + float(16 * pair + 8 * half)
@@ -243,7 +249,7 @@
                     picked[part].append(
                         jnp.where(hit, first[part], jnp.where(hit_next, second[part], 0.0))
                     )
-            base = 8 * tile_y + 16 * pair
+            base = 16 * pair
             for part in range(2):
                 refs[part][base : base + 16, :] = jnp.concatenate(picked[part], 0).astype(BF16)
         refs = (rhs_hi, rhs_lo)
@@ -266,25 +272,14 @@
 
         def product(a, b):
             return lax.dot_general(
-                a[...], b[...], (((1,), (1,)), ((), ())), preferred_element_type=F32
+                a[0 : 8 * tile_y if own_column else tile_y, :], b[...], (((1,), (1,)), ((), ())), preferred_element_type=F32
             )
 
         return product(lhs_hi, rhs_hi) + product(lhs_hi, rhs_lo) + product(lhs_lo, rhs_hi)
 
     width = 3 * NZ
-    acc[:, 0:width] = spread(0)
-
-    @pl.loop(1, n_y)
-    def _(k):
-        mark_copy(k).wait_recv()
-        acc[:, 0:width] += spread(k)
-
-    rim_s[...] = acc[8 * tile_y :, :]
-    rim_copy = pltpu.make_async_remote_copy(
-        src_ref=rim_s, dst_ref=rim_r, send_sem=rim_sem.at[0], recv_sem=rim_sem.at[1],
-        device_id=(right, me_y), device_id_type=MESH,
-    )
-    rim_copy.start()
+    main = 8 * tile_y
+    acc[0:main, 0:width] = spread(0, True)
 
     @pl.loop(0, tiles)
     def _(t):
@@ -292,7 +287,18 @@
         for at, value in enumerate(raw_moments(lambda q: in_v[t, q])):
             mom[t, at] = value
 
-    rim_copy.wait_recv()
+    @pl.loop(1, n_y)
+    def _(k):
+        slot_wait(k)
+        acc[0:main, 0:width] += spread(k, True)
+
+    rim_r[...] = jnp.zeros_like(rim_r)
+
+    @pl.loop(n_y, 2 * n_y)
+    def _(k):
+        slot_wait(k)
+        rim_r[:, 0:width] += spread(k, False)
+
     for y in range(tile_y):
         acc[8 * y : 8 * y + 1, :] += rim_r[y : y + 1, :]
 
@@ -439,9 +445,8 @@
             out[18 + at, 0:1, lanes] = got_p[t, at : at + 1, :]
             out[at, 7:8, lanes] = got_m[t, at : at + 1, :]
 
-    for k in range(1, n_y):
+    for k in range(1, 2 * n_y):
         mark_copy(k).wait_send()
-    rim_copy.wait_send()
     for copy in faces + corners + sides:
         copy.wait_send()
 
@@ -450,7 +455,7 @@
     tiles = populations.shape[2] // LANES
     own = marker_site.shape[1]
     tile_y = 2 * tiles
-    rows = 9 * tile_y
+    rows = 8 * tile_y
     width = 3 * NZ
     dma = pltpu.SemaphoreType.DMA
     hbm = pl.BlockSpec(memory_space=pltpu.HBM)
@@ -465,13 +470,12 @@
             pltpu.VMEM((3, own), F32),
             pltpu.VMEM((tiles, 27, 8, LANES), F32),
             pltpu.VMEM((tiles, 10, 8, LANES), F32),
-            pltpu.VMEM((n_y, 10, own), F32),
+            pltpu.VMEM((2 * n_y, 10, own), F32),
             pltpu.VMEM((rows, own), BF16),
             pltpu.VMEM((rows, own), BF16),
             pltpu.VMEM((width, own), BF16),
             pltpu.VMEM((width, own), BF16),
             pltpu.VMEM((rows, 2 * LANES), F32),
-            pltpu.VMEM((tile_y, 2 * LANES), F32),
             pltpu.VMEM((tile_y, 2 * LANES), F32),
             pltpu.VMEM((27, tiles + 2, 8, LANES), F32),
             pltpu.VMEM((tiles + 2, 9, LANES), F32),
@@ -483,9 +487,8 @@
             pltpu.VMEM((4, 9, LANES), F32),
             dma((3,)),
             dma((tiles,)),
-            dma((n_y,)),
-            dma((n_y,)),
-            dma((2,)),
+            dma((2 * n_y,)),
+            dma((2 * n_y,)),
             dma((4, 3)),
             dma((4, 3)),
             dma((4,)),

time: 23.6 us -> 22.3 us (0.945)
  Pallas kernels: 21.5 us -> 20.2 us
    pallas_call x1, Pallas kernels: 21.5 us -> 20.2 us  [per_device(): pl.pallas_call(functools.partial(step_kernel, n_x, n_y), out_shape=jax.Sh...]
where the time goes in v3:
time: 22.3 us; the launch traced here: 22.1 us
  Pallas kernels  20.2 us (91%)
  local copies, waits for them, and re-layouts  1.21 us (5%)
  between operations  0.66 us (3%)
    pallas_call x1, Pallas kernels, per_device(): pl.pallas_call(functools.partial(step_kernel, n_x, n_y), out_shape=jax.Sh...  20.2 us
    unnamed x1, local copies, waits for them, and re-layouts  1.21 us

profile of v3, /device:TPU:0, one launch (start us, length us, event | category | flops | bytes accessed | tf_op | source)
XLA Modules:
  0.0 22.1 jit_solution(1186980764454355565)
XLA Ops:
  0.7 20.2 %shard_map.55 = f32[27,8,2048]{2,1,0:T(8,128)S(1)} custom-call(f32[27,8,2048]{2,1,0:T(8,128)} %pop.1, s32[4,512]{1,0:T(4,128)} %site_h.1, f32[3,512]{1,0:T(4,128)} %frac_h.1, f32[3,512]{1,0:T(4,128)} %force_h.1, s32[1]{0:T(128)S(6)} %copy.7.count), custom_call_target="tpu_custom_call" | custom-call | tf_op jit(solution)/shard_map/pallas_call | solution.py:462
  20.9 1.2 %copy.8 = f32[27,8,2048]{2,1,0:T(8,128)} copy(f32[27,8,2048]{2,1,0:T(8,128)S(1)} %shard_map.55) | data formatting | bytes 3538944
